TPU v7x, 32 devices: a whole 2x2x4 slice. The times are simulated.
32 devices in a mesh: chan: 16 (over z, y, core), tm: 2 (over x).
Axes of the slice: x: 2, y: 2, z: 4, core: 2. Of those that a mesh axis runs over, the one named last changes fastest.
Arguments:
- raw_samples: bfloat16 [64, 12288], P('tm', 'chan'), may hold values from -6 to 6
- channel_order: int32 [12288], P('chan'), may hold values from 0 to 12287, as said below
- conv_weight: bfloat16 [32, 81], replicated, may hold values from -0.625 to 0.625
- conv_bias: float32 [32], replicated, may hold values from -3 to 3
- taps: bfloat16 [255], replicated, may hold values from -1.5 to 1.5
- shifts: int32 [16, 255], replicated, may hold values from -8 to 8, as said below
Outputs:
- coherence: float32 [16, 32, 6144], P(None, 'tm', 'chan')
Inputs may be any that keep to these rules, and one draw needn't show every extreme that they name: shifts[v, j] = floor((j - 127) * k_v / 127) for an integer slowness k_v of velocity v between -8 and 8; one velocity has k_v = 8 and another k_v = -8. `channel_order`: a permutation that keeps each channel inside its aligned block of 768 channels.
All inputs are finite; a program needn't handle non-finite values.
Results may differ from a plain program's by a relative error of at most 0.0028.
Values may be sent and summed in bfloat16 or wider, within the bound.
A program may use at most 64 MiB of HBM per device.

v0:
```python
import jax
import jax.numpy as jnp
from jax import lax
from jax.experimental import pallas as pl
from jax.experimental.pallas import tpu as pltpu
from jax.sharding import PartitionSpec as P

F = 32
TAPS = 255
KS = 9
SMAX = 8
HALF = 127
BLOCK = 128


def extended_2(value, sides, width):
    for axis, dim in sides:
        devices, length = (lax.axis_size(axis), value.shape[dim])
        up = [(i, (i + 1) % devices) for i in range(devices - 1)]
        down = [(j, i) for i, j in up]
        last = lax.slice_in_dim(value, length - width, length, axis=dim)
        first = lax.slice_in_dim(value, 0, width, axis=dim)
        before = lax.ppermute(last, axis, up)
        after = lax.ppermute(first, axis, down)
        value = jnp.concatenate([before, value, after], axis=dim)
    return value


def lag_weights(taps, shifts):
    rev_taps = jnp.pad(taps[::-1], (1, 0))
    rev_shifts = jnp.pad(shifts.T[::-1], ((1, 0), (0, 0)))
    lag_values = jnp.arange(2 * SMAX + 1, dtype=jnp.int32) - SMAX
    matches = rev_shifts[None, :, :] == lag_values[:, None, None]
    return jnp.where(matches, rev_taps[None, :, None], jnp.zeros((), jnp.bfloat16))


def correlate_kernel(own_ref, ext_ref, weight_ref, out_ref, band_ref):
    time = pl.program_id(0)
    chans = own_ref.shape[2]
    blocks = chans // BLOCK
    width = 2 * BLOCK
    for block in range(blocks):
        own = own_ref[0, :, block * BLOCK : (block + 1) * BLOCK]
        own = (own.astype(jnp.float32) * (1.0 / F)).T.astype(jnp.bfloat16)
        start = (blocks - 1 - block) * BLOCK
        for lag in range(2 * SMAX + 1):
            partner = ext_ref[time + lag, :, start : start + 3 * BLOCK]
            products = jnp.dot(own, partner, preferred_element_type=jnp.float32)
            skewed = pltpu.roll(products, 0, 1, stride=1, stride_axis=0)
            band_ref[block * BLOCK : (block + 1) * BLOCK, lag * width : (lag + 1) * width] = skewed[
                :, BLOCK:
            ].astype(jnp.bfloat16)
    total = jnp.dot(band_ref[...], weight_ref[...], preferred_element_type=jnp.float32)
    out_ref[0] = total.T


def encode_region(padded, out_times, out_chans, conv_weight, conv_bias):
    rows = padded.shape[0]
    pieces = [
        padded[:, col_off % 2, col_off // 2 : col_off // 2 + out_chans] for col_off in range(KS)
    ]
    patches = jnp.concatenate(pieces, axis=0)
    place = (
        jnp.arange(rows)[None, None, :]
        == 2 * jnp.arange(out_times)[:, None, None] + jnp.arange(KS)[None, :, None]
    ).astype(jnp.bfloat16)
    kernel = conv_weight.reshape(-1, KS, KS)
    spread = jnp.einsum("fpq,tpr->tfqr", kernel, place, preferred_element_type=jnp.float32)
    spread = spread.astype(jnp.bfloat16).reshape(-1, KS * rows)
    summed = jnp.dot(spread, patches, preferred_element_type=jnp.float32)
    summed = summed.reshape(out_times, -1, out_chans) + conv_bias[None, :, None]
    return jnp.tanh(summed).astype(jnp.bfloat16)


def body(raw_samples, channel_order, conv_weight, conv_bias, taps, shifts):
    local_times = raw_samples.shape[0] // 2
    local_chans = raw_samples.shape[1] // 2
    local_index = channel_order - lax.axis_index("chan") * raw_samples.shape[1]
    local_index = local_index.reshape(local_chans, 2).T.reshape(-1)
    ordered = jnp.take(raw_samples, local_index, axis=1).reshape(-1, 2, local_chans)
    padded = extended_2(ordered, (("chan", 2),), KS // 4)
    padded = extended_2(padded, (("tm", 0),), KS // 2)
    features = encode_region(padded, local_times, local_chans, conv_weight, conv_bias)
    extended = extended_2(features, (("chan", 2),), HALF)
    extended = extended_2(extended, (("tm", 0),), SMAX)
    extended = jnp.pad(extended, ((0, 0), (0, 0), (0, 2)))[:, :, ::-1]
    vel_count = shifts.shape[0]
    weights = lag_weights(taps, shifts).reshape(-1, vel_count)
    summed = pl.pallas_call(
        correlate_kernel,
        grid=(local_times,),
        in_specs=[
            pl.BlockSpec((1, F, local_chans), lambda t: (t, 0, 0)),
            pl.BlockSpec(extended.shape, lambda t: (0, 0, 0)),
            pl.BlockSpec(weights.shape, lambda t: (0, 0)),
        ],
        out_specs=pl.BlockSpec((1, vel_count, local_chans), lambda t: (t, 0, 0)),
        out_shape=jax.ShapeDtypeStruct((local_times, vel_count, local_chans), jnp.float32),
        scratch_shapes=[pltpu.VMEM((local_chans, weights.shape[0]), jnp.bfloat16)],
        compiler_params=pltpu.CompilerParams(vmem_limit_bytes=40 * 1024 * 1024),
    )(features, extended, weights)
    return summed.transpose(1, 0, 2)


def solution(mesh):
    placed = (P("tm", "chan"), P("chan"), P(), P(), P(), P())
    return jax.shard_map(
        body, mesh=mesh, in_specs=placed, out_specs=P(None, "tm", "chan"), check_vma=False
    )
```

profile of v0, /device:TPU:26, one launch (start us, length us, event | category | flops | bytes accessed | tf_op | source)
XLA Modules:
  0.0 89.4 jit_solution(7992618103191841631)
XLA Ops:
  0.0 1.0 %copy.25 = bf16[32,768]{0,1:T(8,128)(2,1)S(1)} copy(bf16[32,768]{1,0:T(8,128)(2,1)} %param.6) | data formatting | bytes 98304 | tf_op args[0]
  1.0 0.7 broadcast_subtract_fusion
  1.7 0.2 reshape.94
  2.1 1.9 %gather_fusion = bf16[768,32]{1,0:T(8,128)(2,1)S(1)} fusion(bf16[32,768]{0,1:T(8,128)(2,1)S(1)} %copy.25, s32[1024]{0:T(1024)S(1)} %pad_clamp_fusion), kind=kCustom, calls=%fused_computation | custom fusion | bytes 101376 | tf_op jit(solution)/shard_map/jit(_take)/gather | solution.py:80
  4.0 0.1 copy.27
  4.3 2.7 %collective-permute-start.1 = (bf16[32,2,2]{2,0,1:T(8,128)(2,1)S(1)}, bf16[32,2,2]{2,0,1:T(8,128)(2,1)S(1)}, u32[]{:S(2)}, u32[]{:S(2)}) collective-permute-start(bf16[32,2,2]{2,0,1:T(8,128)(2,1)S(1)} %get-tuple-element.12), channel_id=1, source_target_pairs={{2,0},{4,2},{6,4},{8,6},{10,8},{12,10},{14,12},{16,14},{18,16},{20... | collective-permute-start | bytes 776 | tf_op jit(solution)/shard_map/ppermute | solution.py:24
  7.1 1.9 %collective-permute-start = (bf16[32,2,2]{2,0,1:T(8,128)(2,1)S(1)}, bf16[32,2,2]{2,0,1:T(8,128)(2,1)S(1)}, u32[]{:S(2)}, u32[]{:S(2)}) collective-permute-start(bf16[32,2,2]{2,0,1:T(8,128)(2,1)S(1)} %get-tuple-element.11), channel_id=1, source_target_pairs={{0,2},{2,4},{4,6},{6,8},{8,10},{10,12},{12,14},{14,16},{16,18},{18... | collective-permute-start | bytes 776 | tf_op jit(solution)/shard_map/ppermute | solution.py:23
  9.1 0.1 copy.20
  9.2 3.8 %collective-permute-done = bf16[32,2,2]{2,0,1:T(8,128)(2,1)S(1)} collective-permute-done((bf16[32,2,2]{2,0,1:T(8,128)(2,1)S(1)}, bf16[32,2,2]{2,0,1:T(8,128)(2,1)S(1)}, u32[]{:S(2)}, u32[]{:S(2)}) %collective-permute-start) | collective-permute-done | bytes 288 | tf_op jit(solution)/shard_map/ppermute | solution.py:23
  13.1 2.4 %collective-permute-start.3 = (bf16[4,2,388]{2,0,1:T(4,128)(2,1)S(1)}, bf16[4,2,388]{2,0,1:T(4,128)(2,1)S(1)}, u32[]{:S(2)}, u32[]{:S(2)}) collective-permute-start(bf16[4,2,388]{2,0,1:T(4,128)(2,1)S(1)} %get-tuple-element.10), channel_id=1, source_target_pairs={{1,0},{3,2},{5,4},{7,6},{9,8},{11,10},{13,12},{15,14},{17,16},{19,... | collective-permute-start | bytes 18632 | tf_op jit(solution)/shard_map/ppermute | solution.py:24
  15.6 1.3 %collective-permute-start.2 = (bf16[4,2,388]{2,0,1:T(4,128)(2,1)S(1)}, bf16[4,2,388]{2,0,1:T(4,128)(2,1)S(1)}, u32[]{:S(2)}, u32[]{:S(2)}) collective-permute-start(bf16[4,2,388]{2,0,1:T(4,128)(2,1)S(1)} %get-tuple-element.9), channel_id=1, source_target_pairs={{0,1},{2,3},{4,5},{6,7},{8,9},{10,11},{12,13},{14,15},{16,17},{18,... | collective-permute-start | bytes 18632 | tf_op jit(solution)/shard_map/ppermute | solution.py:23
  16.9 0.5 fusion.6
  17.4 0.7 copy.22
  18.1 1.6 %dot_general.9 = bf16[16,32,360]{2,1,0:T(8,128)(2,1)S(1)} reshape(bf16[16,32,9,40]{3,2,1,0:T(8,128)(2,1)S(1)} %copy.22) | data formatting | bytes 737280 | tf_op jit(solution)/shard_map/dot_general | solution.py:70
  19.7 1.4 %collective-permute-done.2 = bf16[4,2,388]{2,0,1:T(4,128)(2,1)S(1)} collective-permute-done((bf16[4,2,388]{2,0,1:T(4,128)(2,1)S(1)}, bf16[4,2,388]{2,0,1:T(4,128)(2,1)S(1)}, u32[]{:S(2)}, u32[]{:S(2)}) %collective-permute-start.2) | collective-permute-done | bytes 6240 | tf_op jit(solution)/shard_map/ppermute | solution.py:23
  21.1 0.1 pad_maximum_fusion.1
  21.9 0.4 fusion.12.own_ref
  22.3 0.1 fusion.30
  22.4 1.9 %collective-permute-start.5 = (bf16[16,32,127]{2,1,0:T(8,128)(2,1)S(1)}, bf16[16,32,127]{2,1,0:T(8,128)(2,1)S(1)}, u32[]{:S(2)}, u32[]{:S(2)}) collective-permute-start(bf16[16,32,127]{2,1,0:T(8,128)(2,1)S(1)} %get-tuple-element.8), channel_id=1, source_target_pairs={{2,0},{4,2},{6,4},{8,6},{10,8},{12,10},{14,12},{16,14},{18,16},{20... | collective-permute-start | bytes 390152 | tf_op jit(solution)/shard_map/ppermute | solution.py:24
  24.3 2.4 %collective-permute-start.4 = (bf16[16,32,127]{2,1,0:T(8,128)(2,1)S(1)}, bf16[16,32,127]{2,1,0:T(8,128)(2,1)S(1)}, u32[]{:S(2)}, u32[]{:S(2)}) collective-permute-start(bf16[16,32,127]{2,1,0:T(8,128)(2,1)S(1)} %get-tuple-element.7), channel_id=1, source_target_pairs={{0,2},{2,4},{4,6},{6,8},{8,10},{10,12},{12,14},{14,16},{16,18},{18... | collective-permute-start | bytes 390152 | tf_op jit(solution)/shard_map/ppermute | solution.py:23
  26.8 4.7 %collective-permute-done.4 = bf16[16,32,127]{2,1,0:T(8,128)(2,1)S(1)} collective-permute-done((bf16[16,32,127]{2,1,0:T(8,128)(2,1)S(1)}, bf16[16,32,127]{2,1,0:T(8,128)(2,1)S(1)}, u32[]{:S(2)}, u32[]{:S(2)}) %collective-permute-start.4) | collective-permute-done | bytes 130080 | tf_op jit(solution)/shard_map/ppermute | solution.py:23
  31.5 0.4 pad_maximum_fusion
  32.0 3.2 %collective-permute-start.7 = (bf16[8,32,638]{2,1,0:T(8,128)(2,1)S(1)}, bf16[8,32,638]{2,1,0:T(8,128)(2,1)S(1)}, u32[]{:S(2)}, u32[]{:S(2)}) collective-permute-start(bf16[8,32,638]{2,1,0:T(8,128)(2,1)S(1)} %get-tuple-element.6), channel_id=1, source_target_pairs={{1,0},{3,2},{5,4},{7,6},{9,8},{11,10},{13,12},{15,14},{17,16},{19,... | collective-permute-start | bytes 979976 | tf_op jit(solution)/shard_map/ppermute | solution.py:24
  35.1 1.3 %collective-permute-start.6 = (bf16[8,32,638]{2,1,0:T(8,128)(2,1)S(1)}, bf16[8,32,638]{2,1,0:T(8,128)(2,1)S(1)}, u32[]{:S(2)}, u32[]{:S(2)}) collective-permute-start(bf16[8,32,638]{2,1,0:T(8,128)(2,1)S(1)} %get-tuple-element.5), channel_id=1, source_target_pairs={{0,1},{2,3},{4,5},{6,7},{8,9},{10,11},{12,13},{14,15},{16,17},{18,... | collective-permute-start | bytes 979976 | tf_op jit(solution)/shard_map/ppermute | solution.py:23
  36.5 0.2 reverse
  37.2 1.2 %fusion.5.weight_ref = bf16[4352,16]{1,0:T(8,128)(2,1)S(1)} fusion(s32[4352]{0:T(1024)S(1)} %eq.39, s32[256,16]{1,0:T(8,128)S(1)} %pad.13.clone, bf16[4352]{0:T(1024)(128)(2,1)S(1)} %broadcast_in_dim.36), kind=kLoop, calls=%fused_computation.8 | loop fusion | flops 139264 | bytes 181760 | tf_op jit(solution)/shard_map/jit(_where)/select_n | solution.py:34
  38.4 1.3 %collective-permute-done.7 = bf16[8,32,638]{2,1,0:T(8,128)(2,1)S(1)} collective-permute-done((bf16[8,32,638]{2,1,0:T(8,128)(2,1)S(1)}, bf16[8,32,638]{2,1,0:T(8,128)(2,1)S(1)}, u32[]{:S(2)}, u32[]{:S(2)}) %collective-permute-start.7) | collective-permute-done | bytes 326688 | tf_op jit(solution)/shard_map/ppermute | solution.py:24
  39.7 4.4 %collective-permute-done.6 = bf16[8,32,638]{2,1,0:T(8,128)(2,1)S(1)} collective-permute-done((bf16[8,32,638]{2,1,0:T(8,128)(2,1)S(1)}, bf16[8,32,638]{2,1,0:T(8,128)(2,1)S(1)}, u32[]{:S(2)}, u32[]{:S(2)}) %collective-permute-start.6) | collective-permute-done | bytes 326688 | tf_op jit(solution)/shard_map/ppermute | solution.py:23
  44.1 1.5 %fusion.8 = bf16[32,32,640]{2,1,0:T(8,128)(2,1)} fusion(bf16[8,32,638]{2,1,0:T(8,128)(2,1)S(1)} %collective-permute-done.7, bf16[8,32,638]{2,1,0:T(8,128)(2,1)S(1)} %collective-permute-done.6, bf16[16,32,127]{2,1,0:T(8,128)(2,1)S(1)} %collective-permute-done.5, bf16[16,32,384]{2,1,0:T(8,128)(2,1)S(1)} %fusion.12.own_ref, ...), kind=kLoop, calls=%fused_computation.12 | loop fusion | flops 10485760 | bytes 2617344 | tf_op jit(solution)/shard_map/concatenate | solution.py:25
  45.6 3.4 %rev.9.ext_ref = bf16[32,32,640]{2,1,0:T(8,128)(2,1)S(1)} reverse(bf16[32,32,640]{2,1,0:T(8,128)(2,1)} %fusion.8), dimensions={2} | reverse | bytes 2621440 | tf_op jit(solution)/shard_map/rev | solution.py:86
  49.0 39.5 %shard_map.64 = f32[16,16,384]{2,1,0:T(8,128)S(1)} custom-call(bf16[16,32,384]{2,1,0:T(8,128)(2,1)S(1)} %fusion.12.own_ref, bf16[32,32,640]{2,1,0:T(8,128)(2,1)S(1)} %rev.9.ext_ref, bf16[4352,16]{1,0:T(8,128)(2,1)S(1)} %fusion.5.weight_ref), custom_call_target="tpu_custom_call" | custom-call | tf_op jit(solution)/shard_map/pallas_call | solution.py:89
  88.5 0.9 copy.29
  (44 shorter events, 1.9 us)
Async XLA Ops:
  0.0 9.1 %copy-start.1 = (bf16[32,81]{1,0:T(8,128)(2,1)S(1)}, bf16[32,81]{1,0:T(8,128)(2,1)}, u32[]{:S(2)}) copy-start(bf16[32,81]{1,0:T(8,128)(2,1)} %param.8) | copy-start | bytes 15556
  4.3 4.9 %collective-permute-start.1 = (bf16[32,2,2]{2,0,1:T(8,128)(2,1)S(1)}, bf16[32,2,2]{2,0,1:T(8,128)(2,1)S(1)}, u32[]{:S(2)}, u32[]{:S(2)}) collective-permute-start(bf16[32,2,2]{2,0,1:T(8,128)(2,1)S(1)} %get-tuple-element.12), channel_id=1, source_target_pairs={{2,0},{4,2},{6,4},{8,6},{10,8},{12,10},{14,12},{16,14},{18,16},{20... | collective-permute-start | bytes 776 | tf_op jit(solution)/shard_map/ppermute | solution.py:24
  7.1 6.0 %collective-permute-start = (bf16[32,2,2]{2,0,1:T(8,128)(2,1)S(1)}, bf16[32,2,2]{2,0,1:T(8,128)(2,1)S(1)}, u32[]{:S(2)}, u32[]{:S(2)}) collective-permute-start(bf16[32,2,2]{2,0,1:T(8,128)(2,1)S(1)} %get-tuple-element.11), channel_id=1, source_target_pairs={{0,2},{2,4},{4,6},{6,8},{8,10},{10,12},{12,14},{14,16},{16,18},{18... | collective-permute-start | bytes 776 | tf_op jit(solution)/shard_map/ppermute | solution.py:23
  13.1 6.6 %collective-permute-start.3 = (bf16[4,2,388]{2,0,1:T(4,128)(2,1)S(1)}, bf16[4,2,388]{2,0,1:T(4,128)(2,1)S(1)}, u32[]{:S(2)}, u32[]{:S(2)}) collective-permute-start(bf16[4,2,388]{2,0,1:T(4,128)(2,1)S(1)} %get-tuple-element.10), channel_id=1, source_target_pairs={{1,0},{3,2},{5,4},{7,6},{9,8},{11,10},{13,12},{15,14},{17,16},{19,... | collective-permute-start | bytes 18632 | tf_op jit(solution)/shard_map/ppermute | solution.py:24
  15.6 5.5 %collective-permute-start.2 = (bf16[4,2,388]{2,0,1:T(4,128)(2,1)S(1)}, bf16[4,2,388]{2,0,1:T(4,128)(2,1)S(1)}, u32[]{:S(2)}, u32[]{:S(2)}) collective-permute-start(bf16[4,2,388]{2,0,1:T(4,128)(2,1)S(1)} %get-tuple-element.9), channel_id=1, source_target_pairs={{0,1},{2,3},{4,5},{6,7},{8,9},{10,11},{12,13},{14,15},{16,17},{18,... | collective-permute-start | bytes 18632 | tf_op jit(solution)/shard_map/ppermute | solution.py:23
  18.1 3.8 %copy-start.2 = (f32[32]{0:T(128)S(1)}, f32[32]{0:T(128)}, u32[]{:S(2)}) copy-start(f32[32]{0:T(128)} %param.9) | copy-start | bytes 388
  22.4 4.4 %collective-permute-start.5 = (bf16[16,32,127]{2,1,0:T(8,128)(2,1)S(1)}, bf16[16,32,127]{2,1,0:T(8,128)(2,1)S(1)}, u32[]{:S(2)}, u32[]{:S(2)}) collective-permute-start(bf16[16,32,127]{2,1,0:T(8,128)(2,1)S(1)} %get-tuple-element.8), channel_id=1, source_target_pairs={{2,0},{4,2},{6,4},{8,6},{10,8},{12,10},{14,12},{16,14},{18,16},{20... | collective-permute-start | bytes 390152 | tf_op jit(solution)/shard_map/ppermute | solution.py:24
  24.3 12.2 %copy-start = (s32[16,255]{1,0:T(8,128)S(1)}, s32[16,255]{1,0:T(8,128)}, u32[]{:S(2)}) copy-start(s32[16,255]{1,0:T(8,128)} %param.11) | copy-start | bytes 48964
  24.3 12.5 %copy-start.3 = (bf16[255]{0:T(256)(128)(2,1)S(1)}, bf16[255]{0:T(256)(128)(2,1)}, u32[]{:S(2)}) copy-start(bf16[255]{0:T(256)(128)(2,1)} %param.10) | copy-start | bytes 1534
  24.3 7.2 %collective-permute-start.4 = (bf16[16,32,127]{2,1,0:T(8,128)(2,1)S(1)}, bf16[16,32,127]{2,1,0:T(8,128)(2,1)S(1)}, u32[]{:S(2)}, u32[]{:S(2)}) collective-permute-start(bf16[16,32,127]{2,1,0:T(8,128)(2,1)S(1)} %get-tuple-element.7), channel_id=1, source_target_pairs={{0,2},{2,4},{4,6},{6,8},{8,10},{10,12},{12,14},{14,16},{16,18},{18... | collective-permute-start | bytes 390152 | tf_op jit(solution)/shard_map/ppermute | solution.py:23
  32.0 7.7 %collective-permute-start.7 = (bf16[8,32,638]{2,1,0:T(8,128)(2,1)S(1)}, bf16[8,32,638]{2,1,0:T(8,128)(2,1)S(1)}, u32[]{:S(2)}, u32[]{:S(2)}) collective-permute-start(bf16[8,32,638]{2,1,0:T(8,128)(2,1)S(1)} %get-tuple-element.6), channel_id=1, source_target_pairs={{1,0},{3,2},{5,4},{7,6},{9,8},{11,10},{13,12},{15,14},{17,16},{19,... | collective-permute-start | bytes 979976 | tf_op jit(solution)/shard_map/ppermute | solution.py:24
  35.1 9.0 %collective-permute-start.6 = (bf16[8,32,638]{2,1,0:T(8,128)(2,1)S(1)}, bf16[8,32,638]{2,1,0:T(8,128)(2,1)S(1)}, u32[]{:S(2)}, u32[]{:S(2)}) collective-permute-start(bf16[8,32,638]{2,1,0:T(8,128)(2,1)S(1)} %get-tuple-element.5), channel_id=1, source_target_pairs={{0,1},{2,3},{4,5},{6,7},{8,9},{10,11},{12,13},{14,15},{16,17},{18,... | collective-permute-start | bytes 979976 | tf_op jit(solution)/shard_map/ppermute | solution.py:23
where the time goes:
time: 90.4 us; the launch traced here: 89.4 us
  Pallas kernels  39.5 us (44%)
  starting transfers between devices  17.2 us (19%)
  waiting for transfers between devices  15.7 us (17%)
  local copies, waits for them, and re-layouts  11.6 us (13%)
  other arithmetic  4.17 us (5%)
  matrix products  0.93 us (1%)
    pallas_call x1, Pallas kernels, body(): pl.pallas_call(correlate_kernel, grid=(local_times,), in_specs=[pl.BlockS...  39.5 us
    ppermute x4, waiting for transfers between devices, extended_2(): before = lax.ppermute(last, axis, up)  14.3 us
    ppermute x4, starting transfers between devices, extended_2(): after = lax.ppermute(first, axis, down)  10.3 us
    ppermute x4, starting transfers between devices, extended_2(): before = lax.ppermute(last, axis, up)  6.91 us
    rev x1, local copies, waits for them, and re-layouts, body(): extended = jnp.pad(extended, ((0, 0), (0, 0), (0, 2)))[:, :, ::-1]  3.38 us
    unnamed x24, local copies, waits for them, and re-layouts  2.16 us
    gather x2, local copies, waits for them, and re-layouts, body(): jnp.take(raw_samples, local_index, axis=1).reshape(-1, 2, local_chans)  2.01 us
    concatenate x3, other arithmetic, extended_2(): value = jnp.concatenate([before, value, after], axis=dim)  1.95 us
  transfers between devices with their start and end apart: 8, of which 6 were waited for; matrix products, arithmetic and copies ran while one was open for 6% of the time, Pallas kernels for 0%

commit v1 on v0

--- a/solution.py
+++ b/solution.py
@@ -78,11 +78,24 @@
     local_index = channel_order - lax.axis_index("chan") * raw_samples.shape[1]
     local_index = local_index.reshape(local_chans, 2).T.reshape(-1)
     ordered = jnp.take(raw_samples, local_index, axis=1).reshape(-1, 2, local_chans)
-    padded = extended_2(ordered, (("chan", 2),), KS // 4)
-    padded = extended_2(padded, (("tm", 0),), KS // 2)
-    features = encode_region(padded, local_times, local_chans, conv_weight, conv_bias)
-    extended = extended_2(features, (("chan", 2),), HALF)
-    extended = extended_2(extended, (("tm", 0),), SMAX)
+    padded = extended_2(ordered, (("chan", 2),), HALF + KS // 4)
+    padded = extended_2(padded, (("tm", 0),), 2 * SMAX + KS // 2)
+    wide = local_chans + 2 * HALF
+    groups = [
+        encode_region(
+            padded[first : first + 2 * local_times + KS - 1],
+            local_times, wide, conv_weight, conv_bias,
+        )
+        for first in range(0, 2 * (local_times + 2 * SMAX), 2 * local_times)
+    ]
+    extended = jnp.concatenate(groups, axis=0)
+    time_at = jnp.arange(local_times + 2 * SMAX) - SMAX + lax.axis_index("tm") * local_times
+    chan_at = jnp.arange(wide) - HALF + lax.axis_index("chan") * local_chans
+    time_in = (time_at >= 0) & (time_at < lax.axis_size("tm") * local_times)
+    chan_in = (chan_at >= 0) & (chan_at < lax.axis_size("chan") * local_chans)
+    inside = time_in[:, None, None] & chan_in[None, None, :]
+    extended = jnp.where(inside, extended, jnp.zeros((), jnp.bfloat16))
+    features = extended[SMAX : SMAX + local_times, :, HALF : HALF + local_chans]
     extended = jnp.pad(extended, ((0, 0), (0, 0), (0, 2)))[:, :, ::-1]
     vel_count = shifts.shape[0]
     weights = lag_weights(taps, shifts).reshape(-1, vel_count)

time: 90.4 us -> 71.9 us (0.80)
  waiting for transfers between devices: 15.7 us -> 3.31 us
  starting transfers between devices: 17.2 us -> 10.5 us
  local copies, waits for them, and re-layouts: 11.6 us -> 13.5 us
  other arithmetic: 4.17 us -> 2.78 us
    ppermute x4 -> x2, waiting for transfers between devices: 14.3 us -> 3.3 us  [extended_2(): before = lax.ppermute(last, axis, up)]
    ppermute x4 -> x2, starting transfers between devices: 6.91 us -> 3.21 us  [extended_2(): before = lax.ppermute(last, axis, up)]
    ppermute x4 -> x2, starting transfers between devices: 10.3 us -> 7.29 us  [extended_2(): after = lax.ppermute(first, axis, down)]
    concatenate x3 -> x2, other arithmetic: 1.95 us -> 0.23 us  [extended_2(): value = jnp.concatenate([before, value, after], axis=dim)]
    ppermute x4 -> x2, waiting for transfers between devices: 1.36 us -> 0.01 us  [extended_2(): after = lax.ppermute(first, axis, down)]
    pad x0 -> x1, local copies, waits for them, and re-layouts: none -> 1.2 us  [body(): extended = jnp.pad(extended, ((0, 0), (0, 0), (0, 2)))[:, :, ::-1]]
    unnamed x24 -> x32, local copies, waits for them, and re-layouts: 2.16 us -> 2.81 us
  transfers between devices with their start and end apart: 8 -> 4, of which waited for: 6 -> 1; matrix products, arithmetic and copies ran while one was open for 6% -> 7% of each run, Pallas kernels for 0% -> 0%
where the time goes in v1:
time: 71.9 us; the launch traced here: 71.6 us
  Pallas kernels  39.5 us (55%)
  local copies, waits for them, and re-layouts  13.5 us (19%)
  starting transfers between devices  10.5 us (15%)
  waiting for transfers between devices  3.31 us (5%)
  other arithmetic  2.78 us (4%)
  matrix products  1.59 us (2%)
    pallas_call x1, Pallas kernels, body(): pl.pallas_call(correlate_kernel, grid=(local_times,), in_specs=[pl.BlockS...  39.5 us
    ppermute x2, starting transfers between devices, extended_2(): after = lax.ppermute(first, axis, down)  7.29 us
    rev x1, local copies, waits for them, and re-layouts, body(): extended = jnp.pad(extended, ((0, 0), (0, 0), (0, 2)))[:, :, ::-1]  3.38 us
    ppermute x2, waiting for transfers between devices, extended_2(): before = lax.ppermute(last, axis, up)  3.3 us
    ppermute x2, starting transfers between devices, extended_2(): before = lax.ppermute(last, axis, up)  3.21 us
    unnamed x32, local copies, waits for them, and re-layouts  2.81 us
    gather x2, local copies, waits for them, and re-layouts, body(): jnp.take(raw_samples, local_index, axis=1).reshape(-1, 2, local_chans)  2.01 us
    dot_general x1, local copies, waits for them, and re-layouts, encode_region(): summed = jnp.dot(spread, patches, preferred_element_type=jnp.float32)  1.57 us
  transfers between devices with their start and end apart: 4, of which 1 were waited for; matrix products, arithmetic and copies ran while one was open for 7% of the time, Pallas kernels for 0%

profile of v1, /device:TPU:26, one launch (start us, length us, event | category | flops | bytes accessed | tf_op | source)
XLA Modules:
  0.0 71.6 jit_solution(17351947985302789440)
XLA Ops:
  0.0 1.0 %copy.25 = bf16[32,768]{0,1:T(8,128)(2,1)S(1)} copy(bf16[32,768]{1,0:T(8,128)(2,1)} %param.6) | data formatting | bytes 98304 | tf_op args[0]
  1.0 0.7 broadcast_subtract_fusion
  1.7 0.2 reshape.145
  2.1 1.9 %gather_fusion = bf16[768,32]{1,0:T(8,128)(2,1)S(1)} fusion(bf16[32,768]{0,1:T(8,128)(2,1)S(1)} %copy.25, s32[1024]{0:T(1024)S(1)} %pad_clamp_fusion), kind=kCustom, calls=%fused_computation | custom fusion | bytes 101376 | tf_op jit(solution)/shard_map/jit(_take)/gather | solution.py:80
  4.0 0.1 copy.27
  4.1 0.1 copy.23
  4.3 2.7 %collective-permute-start.1 = (bf16[32,2,129]{2,0,1:T(8,128)(2,1)S(1)}, bf16[32,2,129]{2,0,1:T(8,128)(2,1)S(1)}, u32[]{:S(2)}, u32[]{:S(2)}) collective-permute-start(bf16[32,2,129]{2,0,1:T(8,128)(2,1)S(1)} %get-tuple-element.10), channel_id=1, source_target_pairs={{2,0},{4,2},{6,4},{8,6},{10,8},{12,10},{14,12},{16,14},{18,16},{20... | collective-permute-start | bytes 49544 | tf_op jit(solution)/shard_map/ppermute | solution.py:24
  7.1 1.9 %collective-permute-start = (bf16[32,2,129]{2,0,1:T(8,128)(2,1)S(1)}, bf16[32,2,129]{2,0,1:T(8,128)(2,1)S(1)}, u32[]{:S(2)}, u32[]{:S(2)}) collective-permute-start(bf16[32,2,129]{2,0,1:T(8,128)(2,1)S(1)} %get-tuple-element.9), channel_id=1, source_target_pairs={{0,2},{2,4},{4,6},{6,8},{8,10},{10,12},{12,14},{14,16},{16,18},{18... | collective-permute-start | bytes 49544 | tf_op jit(solution)/shard_map/ppermute | solution.py:23
  9.1 0.1 copy.20
  9.3 0.5 fusion.3
  9.9 3.3 %collective-permute-done = bf16[32,2,129]{2,0,1:T(8,128)(2,1)S(1)} collective-permute-done((bf16[32,2,129]{2,0,1:T(8,128)(2,1)S(1)}, bf16[32,2,129]{2,0,1:T(8,128)(2,1)S(1)}, u32[]{:S(2)}, u32[]{:S(2)}) %collective-permute-start) | collective-permute-done | bytes 16544 | tf_op jit(solution)/shard_map/ppermute | solution.py:23
  13.3 1.3 %collective-permute-start.2 = (bf16[20,2,642]{2,0,1:T(8,128)(2,1)S(1)}, bf16[20,2,642]{2,0,1:T(8,128)(2,1)S(1)}, u32[]{:S(2)}, u32[]{:S(2)}) collective-permute-start(bf16[20,2,642]{2,0,1:T(8,128)(2,1)S(1)} %get-tuple-element.7), channel_id=1, source_target_pairs={{0,1},{2,3},{4,5},{6,7},{8,9},{10,11},{12,13},{14,15},{16,17},{18,... | collective-permute-start | bytes 154088 | tf_op jit(solution)/shard_map/ppermute | solution.py:23
  14.6 4.5 %collective-permute-start.3 = (bf16[20,2,642]{2,0,1:T(8,128)(2,1)S(1)}, bf16[20,2,642]{2,0,1:T(8,128)(2,1)S(1)}, u32[]{:S(2)}, u32[]{:S(2)}) collective-permute-start(bf16[20,2,642]{2,0,1:T(8,128)(2,1)S(1)} %get-tuple-element.8), channel_id=1, source_target_pairs={{1,0},{3,2},{5,4},{7,6},{9,8},{11,10},{13,12},{15,14},{17,16},{19,... | collective-permute-start | bytes 154088 | tf_op jit(solution)/shard_map/ppermute | solution.py:24
  19.2 0.7 copy.22
  19.9 1.6 %dot_general.13 = bf16[16,32,360]{2,1,0:T(8,128)(2,1)S(1)} reshape(bf16[16,32,9,40]{3,2,1,0:T(8,128)(2,1)S(1)} %copy.22) | data formatting | bytes 737280 | tf_op jit(solution)/shard_map/dot_general | solution.py:70
  21.6 0.2 reverse
  21.8 0.1 copy.33
  22.0 0.1 reverse.1
  22.3 1.2 %fusion.weight_ref = bf16[4352,16]{1,0:T(8,128)(2,1)S(1)} fusion(s32[4352]{0:T(1024)S(1)} %eq.46, s32[256,16]{1,0:T(8,128)S(1)} %pad.13.clone, bf16[4352]{0:T(1024)(128)(2,1)S(1)} %broadcast_in_dim.56), kind=kLoop, calls=%fused_computation.2 | loop fusion | flops 139264 | bytes 181760 | tf_op jit(solution)/shard_map/jit(_where)/select_n | solution.py:34
  23.5 0.1 maximum_maximum_fusion
  24.0 0.1 fusion.14
  24.1 0.1 fusion.13
  24.2 0.1 fusion.12
  24.9 0.1 fusion.11
  25.0 0.5 fusion.5
  25.5 0.5 fusion.4
  26.1 0.3 maximum_select_fusion
  26.4 0.2 slice.138.own_ref
  26.6 1.2 %pad.12 = bf16[32,32,640]{2,1,0:T(8,128)(2,1)} pad(bf16[32,32,638]{2,1,0:T(8,128)(2,1)S(1)} %maximum_select_fusion, bf16[]{:T(256)} %constant.48.clone.1), padding=0_0x0_0x0_2 | pad | bytes 2617346 | tf_op jit(solution)/shard_map/jit(_pad)/pad | solution.py:99
  27.8 3.4 %rev.9.ext_ref = bf16[32,32,640]{2,1,0:T(8,128)(2,1)S(1)} reverse(bf16[32,32,640]{2,1,0:T(8,128)(2,1)} %pad.12), dimensions={2} | reverse | bytes 2621440 | tf_op jit(solution)/shard_map/rev | solution.py:99
  31.2 39.5 %shard_map.64 = f32[16,16,384]{2,1,0:T(8,128)S(1)} custom-call(bf16[16,32,384]{2,1,0:T(8,128)(2,1)S(1)} %slice.138.own_ref, bf16[32,32,640]{2,1,0:T(8,128)(2,1)S(1)} %rev.9.ext_ref, bf16[4352,16]{1,0:T(8,128)(2,1)S(1)} %fusion.weight_ref), custom_call_target="tpu_custom_call" | custom-call | tf_op jit(solution)/shard_map/pallas_call | solution.py:102
  70.7 0.9 %copy.29 = f32[16,16,384]{2,1,0:T(8,128)} copy(f32[16,16,384]{2,0,1:T(8,128)S(1)} %bitcast.109) | data formatting | bytes 786432 | tf_op jit(solution)/shard_map/transpose | solution.py:115
  (48 shorter events, 1.9 us)
Async XLA Ops:
  0.0 9.1 %copy-start.1 = (bf16[32,81]{1,0:T(8,128)(2,1)S(1)}, bf16[32,81]{1,0:T(8,128)(2,1)}, u32[]{:S(2)}) copy-start(bf16[32,81]{1,0:T(8,128)(2,1)} %param.8) | copy-start | bytes 15556
  4.3 5.6 %collective-permute-start.1 = (bf16[32,2,129]{2,0,1:T(8,128)(2,1)S(1)}, bf16[32,2,129]{2,0,1:T(8,128)(2,1)S(1)}, u32[]{:S(2)}, u32[]{:S(2)}) collective-permute-start(bf16[32,2,129]{2,0,1:T(8,128)(2,1)S(1)} %get-tuple-element.10), channel_id=1, source_target_pairs={{2,0},{4,2},{6,4},{8,6},{10,8},{12,10},{14,12},{16,14},{18,16},{20... | collective-permute-start | bytes 49544 | tf_op jit(solution)/shard_map/ppermute | solution.py:24
  7.1 6.1 %collective-permute-start = (bf16[32,2,129]{2,0,1:T(8,128)(2,1)S(1)}, bf16[32,2,129]{2,0,1:T(8,128)(2,1)S(1)}, u32[]{:S(2)}, u32[]{:S(2)}) collective-permute-start(bf16[32,2,129]{2,0,1:T(8,128)(2,1)S(1)} %get-tuple-element.9), channel_id=1, source_target_pairs={{0,2},{2,4},{4,6},{6,8},{8,10},{10,12},{12,14},{14,16},{16,18},{18... | collective-permute-start | bytes 49544 | tf_op jit(solution)/shard_map/ppermute | solution.py:23
  13.3 10.1 %collective-permute-start.2 = (bf16[20,2,642]{2,0,1:T(8,128)(2,1)S(1)}, bf16[20,2,642]{2,0,1:T(8,128)(2,1)S(1)}, u32[]{:S(2)}, u32[]{:S(2)}) collective-permute-start(bf16[20,2,642]{2,0,1:T(8,128)(2,1)S(1)} %get-tuple-element.7), channel_id=1, source_target_pairs={{0,1},{2,3},{4,5},{6,7},{8,9},{10,11},{12,13},{14,15},{16,17},{18,... | collective-permute-start | bytes 154088 | tf_op jit(solution)/shard_map/ppermute | solution.py:23
  14.6 8.8 %collective-permute-start.3 = (bf16[20,2,642]{2,0,1:T(8,128)(2,1)S(1)}, bf16[20,2,642]{2,0,1:T(8,128)(2,1)S(1)}, u32[]{:S(2)}, u32[]{:S(2)}) collective-permute-start(bf16[20,2,642]{2,0,1:T(8,128)(2,1)S(1)} %get-tuple-element.8), channel_id=1, source_target_pairs={{1,0},{3,2},{5,4},{7,6},{9,8},{11,10},{13,12},{15,14},{17,16},{19,... | collective-permute-start | bytes 154088 | tf_op jit(solution)/shard_map/ppermute | solution.py:24
  19.9 1.7 %copy-start = (s32[16,255]{1,0:T(8,128)S(1)}, s32[16,255]{1,0:T(8,128)}, u32[]{:S(2)}) copy-start(s32[16,255]{1,0:T(8,128)} %param.11) | copy-start | bytes 48964
  19.9 2.0 %copy-start.2 = (bf16[255]{0:T(256)(128)(2,1)S(1)}, bf16[255]{0:T(256)(128)(2,1)}, u32[]{:S(2)}) copy-start(bf16[255]{0:T(256)(128)(2,1)} %param.10) | copy-start | bytes 1534
  23.5 1.5 %copy-start.3 = (f32[32]{0:T(128)S(1)}, f32[32]{0:T(128)}, u32[]{:S(2)}) copy-start(f32[32]{0:T(128)} %param.9) | copy-start | bytes 388

commit v2 on v1

--- a/solution.py
+++ b/solution.py
@@ -34,8 +34,21 @@
     return jnp.where(matches, rev_taps[None, :, None], jnp.zeros((), jnp.bfloat16))
 
 
-def correlate_kernel(own_ref, ext_ref, weight_ref, out_ref, band_ref):
+def correlate_kernel(own_ref, raw_ref, weight_ref, out_ref, band_ref, ext_ref):
     time = pl.program_id(0)
+
+    @pl.when(time == 0)
+    def _():
+        rows = lax.broadcasted_iota(jnp.int32, (BLOCK, BLOCK), 0)
+        cols = lax.broadcasted_iota(jnp.int32, (BLOCK, BLOCK), 1)
+        flip = (rows + cols == BLOCK - 1).astype(jnp.float32).astype(jnp.bfloat16)
+        times, feats, wide = raw_ref.shape
+        for first in range(0, wide, BLOCK):
+            part = raw_ref[:, :, first : first + BLOCK].reshape(times * feats, BLOCK)
+            part = jnp.dot(part, flip, preferred_element_type=jnp.float32)
+            last = wide - BLOCK - first
+            ext_ref[:, :, last : last + BLOCK] = part.astype(jnp.bfloat16).reshape(times, feats, BLOCK)
+
     chans = own_ref.shape[2]
     blocks = chans // BLOCK
     width = 2 * BLOCK
@@ -96,7 +109,7 @@
     inside = time_in[:, None, None] & chan_in[None, None, :]
     extended = jnp.where(inside, extended, jnp.zeros((), jnp.bfloat16))
     features = extended[SMAX : SMAX + local_times, :, HALF : HALF + local_chans]
-    extended = jnp.pad(extended, ((0, 0), (0, 0), (0, 2)))[:, :, ::-1]
+    extended = jnp.pad(extended, ((0, 0), (0, 0), (0, 2)))
     vel_count = shifts.shape[0]
     weights = lag_weights(taps, shifts).reshape(-1, vel_count)
     summed = pl.pallas_call(
@@ -109,7 +122,10 @@
         ],
         out_specs=pl.BlockSpec((1, vel_count, local_chans), lambda t: (t, 0, 0)),
         out_shape=jax.ShapeDtypeStruct((local_times, vel_count, local_chans), jnp.float32),
-        scratch_shapes=[pltpu.VMEM((local_chans, weights.shape[0]), jnp.bfloat16)],
+        scratch_shapes=[
+            pltpu.VMEM((local_chans, weights.shape[0]), jnp.bfloat16),
+            pltpu.VMEM(extended.shape, jnp.bfloat16),
+        ],
         compiler_params=pltpu.CompilerParams(vmem_limit_bytes=40 * 1024 * 1024),
     )(features, extended, weights)
     return summed.transpose(1, 0, 2)

time: 71.9 us -> 67.9 us (0.944)
  local copies, waits for them, and re-layouts: 13.5 us -> 9.07 us
    rev x1 -> x0, local copies, waits for them, and re-layouts: 3.38 us -> none  [body(): extended = jnp.pad(extended, ((0, 0), (0, 0), (0, 2)))[:, :, ::-1]]
    pad x1, local copies, waits for them, and re-layouts: 1.2 us -> 0.12 us  [body(): extended = jnp.pad(extended, ((0, 0), (0, 0), (0, 2)))]
where the time goes in v2:
time: 67.9 us; the launch traced here: 67.6 us
  Pallas kernels  40 us (59%)
  starting transfers between devices  10.5 us (15%)
  local copies, waits for them, and re-layouts  9.07 us (13%)
  waiting for transfers between devices  3.31 us (5%)
  other arithmetic  2.78 us (4%)
  matrix products  1.59 us (2%)
    pallas_call x1, Pallas kernels, body(): pl.pallas_call(correlate_kernel, grid=(local_times,), in_specs=[pl.BlockS...  40 us
    ppermute x2, starting transfers between devices, extended_2(): after = lax.ppermute(first, axis, down)  7.29 us
    ppermute x2, waiting for transfers between devices, extended_2(): before = lax.ppermute(last, axis, up)  3.3 us
    ppermute x2, starting transfers between devices, extended_2(): before = lax.ppermute(last, axis, up)  3.21 us
    unnamed x32, local copies, waits for them, and re-layouts  2.81 us
    gather x2, local copies, waits for them, and re-layouts, body(): jnp.take(raw_samples, local_index, axis=1).reshape(-1, 2, local_chans)  2.01 us
    dot_general x1, local copies, waits for them, and re-layouts, encode_region(): summed = jnp.dot(spread, patches, preferred_element_type=jnp.float32)  1.57 us
  transfers between devices with their start and end apart: 4, of which 1 were waited for; matrix products, arithmetic and copies ran while one was open for 7% of the time, Pallas kernels for 0%

profile of v2, /device:TPU:26, one launch (start us, length us, event | category | flops | bytes accessed | tf_op | source)
XLA Modules:
  0.0 67.6 jit_solution(10389714772417629918)
XLA Ops:
  0.0 1.0 %copy.25 = bf16[32,768]{0,1:T(8,128)(2,1)S(1)} copy(bf16[32,768]{1,0:T(8,128)(2,1)} %param.6) | data formatting | bytes 98304 | tf_op args[0]
  1.0 0.7 %broadcast_subtract_fusion = s32[768]{0:T(1024)S(1)} fusion(s32[768]{0:T(1024)} %param.7, s32[]{:T(128)S(6)} %mul.21), kind=kLoop, calls=%fused_computation.70 | loop fusion | flops 768 | bytes 6148 | tf_op jit(solution)/shard_map/sub | solution.py:91
  1.7 0.2 reshape.145
  2.1 1.9 %gather_fusion = bf16[768,32]{1,0:T(8,128)(2,1)S(1)} fusion(bf16[32,768]{0,1:T(8,128)(2,1)S(1)} %copy.25, s32[1024]{0:T(1024)S(1)} %pad_clamp_fusion), kind=kCustom, calls=%fused_computation | custom fusion | bytes 101376 | tf_op jit(solution)/shard_map/jit(_take)/gather | solution.py:93
  4.0 0.1 copy.27
  4.1 0.1 copy.23
  4.3 2.7 %collective-permute-start.1 = (bf16[32,2,129]{2,0,1:T(8,128)(2,1)S(1)}, bf16[32,2,129]{2,0,1:T(8,128)(2,1)S(1)}, u32[]{:S(2)}, u32[]{:S(2)}) collective-permute-start(bf16[32,2,129]{2,0,1:T(8,128)(2,1)S(1)} %get-tuple-element.10), channel_id=1, source_target_pairs={{2,0},{4,2},{6,4},{8,6},{10,8},{12,10},{14,12},{16,14},{18,16},{20... | collective-permute-start | bytes 49544 | tf_op jit(solution)/shard_map/ppermute | solution.py:24
  7.1 1.9 %collective-permute-start = (bf16[32,2,129]{2,0,1:T(8,128)(2,1)S(1)}, bf16[32,2,129]{2,0,1:T(8,128)(2,1)S(1)}, u32[]{:S(2)}, u32[]{:S(2)}) collective-permute-start(bf16[32,2,129]{2,0,1:T(8,128)(2,1)S(1)} %get-tuple-element.9), channel_id=1, source_target_pairs={{0,2},{2,4},{4,6},{6,8},{8,10},{10,12},{12,14},{14,16},{16,18},{18... | collective-permute-start | bytes 49544 | tf_op jit(solution)/shard_map/ppermute | solution.py:23
  9.1 0.1 copy.20
  9.3 0.5 fusion.3
  9.9 3.3 %collective-permute-done = bf16[32,2,129]{2,0,1:T(8,128)(2,1)S(1)} collective-permute-done((bf16[32,2,129]{2,0,1:T(8,128)(2,1)S(1)}, bf16[32,2,129]{2,0,1:T(8,128)(2,1)S(1)}, u32[]{:S(2)}, u32[]{:S(2)}) %collective-permute-start) | collective-permute-done | bytes 16544 | tf_op jit(solution)/shard_map/ppermute | solution.py:23
  13.3 1.3 %collective-permute-start.2 = (bf16[20,2,642]{2,0,1:T(8,128)(2,1)S(1)}, bf16[20,2,642]{2,0,1:T(8,128)(2,1)S(1)}, u32[]{:S(2)}, u32[]{:S(2)}) collective-permute-start(bf16[20,2,642]{2,0,1:T(8,128)(2,1)S(1)} %get-tuple-element.7), channel_id=1, source_target_pairs={{0,1},{2,3},{4,5},{6,7},{8,9},{10,11},{12,13},{14,15},{16,17},{18,... | collective-permute-start | bytes 154088 | tf_op jit(solution)/shard_map/ppermute | solution.py:23
  14.6 4.5 %collective-permute-start.3 = (bf16[20,2,642]{2,0,1:T(8,128)(2,1)S(1)}, bf16[20,2,642]{2,0,1:T(8,128)(2,1)S(1)}, u32[]{:S(2)}, u32[]{:S(2)}) collective-permute-start(bf16[20,2,642]{2,0,1:T(8,128)(2,1)S(1)} %get-tuple-element.8), channel_id=1, source_target_pairs={{1,0},{3,2},{5,4},{7,6},{9,8},{11,10},{13,12},{15,14},{17,16},{19,... | collective-permute-start | bytes 154088 | tf_op jit(solution)/shard_map/ppermute | solution.py:24
  19.2 0.7 %copy.22 = bf16[16,32,9,40]{3,2,1,0:T(8,128)(2,1)S(1)} copy(bf16[16,32,9,40]{3,1,2,0:T(8,128)(2,1)S(1)} %fusion.3) | data formatting | bytes 737280 | tf_op jit(solution)/shard_map/convert_element_type | solution.py:82
  19.9 1.6 %dot_general.13 = bf16[16,32,360]{2,1,0:T(8,128)(2,1)S(1)} reshape(bf16[16,32,9,40]{3,2,1,0:T(8,128)(2,1)S(1)} %copy.22) | data formatting | bytes 737280 | tf_op jit(solution)/shard_map/dot_general | solution.py:83
  21.6 0.2 reverse
  21.8 0.1 copy.33
  21.9 0.1 reverse.1
  22.3 1.2 %fusion.weight_ref = bf16[4352,16]{1,0:T(8,128)(2,1)S(1)} fusion(s32[4352]{0:T(1024)S(1)} %eq.46, s32[256,16]{1,0:T(8,128)S(1)} %pad.13.clone, bf16[4352]{0:T(1024)(128)(2,1)S(1)} %broadcast_in_dim.56), kind=kLoop, calls=%fused_computation.2 | loop fusion | flops 139264 | bytes 181760 | tf_op jit(solution)/shard_map/jit(_where)/select_n | solution.py:34
  23.5 0.1 maximum_maximum_fusion
  23.7 0.1 fusion.17
  23.8 0.1 fusion.16
  23.9 0.1 fusion.15
  24.0 0.1 fusion.14
  24.9 0.1 fusion.11
  25.0 0.5 fusion.5
  25.5 0.5 fusion.4
  26.1 0.3 maximum_select_fusion
  26.4 0.2 slice.138.own_ref
  26.6 0.1 pad.12.raw_ref
  26.7 40.0 %shard_map.64 = f32[16,16,384]{2,1,0:T(8,128)S(1)} custom-call(bf16[16,32,384]{2,1,0:T(8,128)(2,1)S(1)} %slice.138.own_ref, bf16[32,32,640]{2,1,0:T(8,128)(2,1)S(1)} %pad.12.raw_ref, bf16[4352,16]{1,0:T(8,128)(2,1)S(1)} %fusion.weight_ref), custom_call_target="tpu_custom_call" | custom-call | tf_op jit(solution)/shard_map/pallas_call | solution.py:115
  66.8 0.9 %copy.29 = f32[16,16,384]{2,1,0:T(8,128)} copy(f32[16,16,384]{2,0,1:T(8,128)S(1)} %bitcast.109) | data formatting | bytes 786432 | tf_op jit(solution)/shard_map/transpose | solution.py:131
  (47 shorter events, 1.8 us)
Async XLA Ops:
  0.0 9.1 %copy-start.1 = (bf16[32,81]{1,0:T(8,128)(2,1)S(1)}, bf16[32,81]{1,0:T(8,128)(2,1)}, u32[]{:S(2)}) copy-start(bf16[32,81]{1,0:T(8,128)(2,1)} %param.8) | copy-start | bytes 15556
  4.3 5.6 %collective-permute-start.1 = (bf16[32,2,129]{2,0,1:T(8,128)(2,1)S(1)}, bf16[32,2,129]{2,0,1:T(8,128)(2,1)S(1)}, u32[]{:S(2)}, u32[]{:S(2)}) collective-permute-start(bf16[32,2,129]{2,0,1:T(8,128)(2,1)S(1)} %get-tuple-element.10), channel_id=1, source_target_pairs={{2,0},{4,2},{6,4},{8,6},{10,8},{12,10},{14,12},{16,14},{18,16},{20... | collective-permute-start | bytes 49544 | tf_op jit(solution)/shard_map/ppermute | solution.py:24
  7.1 6.1 %collective-permute-start = (bf16[32,2,129]{2,0,1:T(8,128)(2,1)S(1)}, bf16[32,2,129]{2,0,1:T(8,128)(2,1)S(1)}, u32[]{:S(2)}, u32[]{:S(2)}) collective-permute-start(bf16[32,2,129]{2,0,1:T(8,128)(2,1)S(1)} %get-tuple-element.9), channel_id=1, source_target_pairs={{0,2},{2,4},{4,6},{6,8},{8,10},{10,12},{12,14},{14,16},{16,18},{18... | collective-permute-start | bytes 49544 | tf_op jit(solution)/shard_map/ppermute | solution.py:23
  13.3 10.1 %collective-permute-start.2 = (bf16[20,2,642]{2,0,1:T(8,128)(2,1)S(1)}, bf16[20,2,642]{2,0,1:T(8,128)(2,1)S(1)}, u32[]{:S(2)}, u32[]{:S(2)}) collective-permute-start(bf16[20,2,642]{2,0,1:T(8,128)(2,1)S(1)} %get-tuple-element.7), channel_id=1, source_target_pairs={{0,1},{2,3},{4,5},{6,7},{8,9},{10,11},{12,13},{14,15},{16,17},{18,... | collective-permute-start | bytes 154088 | tf_op jit(solution)/shard_map/ppermute | solution.py:23
  14.6 8.8 %collective-permute-start.3 = (bf16[20,2,642]{2,0,1:T(8,128)(2,1)S(1)}, bf16[20,2,642]{2,0,1:T(8,128)(2,1)S(1)}, u32[]{:S(2)}, u32[]{:S(2)}) collective-permute-start(bf16[20,2,642]{2,0,1:T(8,128)(2,1)S(1)} %get-tuple-element.8), channel_id=1, source_target_pairs={{1,0},{3,2},{5,4},{7,6},{9,8},{11,10},{13,12},{15,14},{17,16},{19,... | collective-permute-start | bytes 154088 | tf_op jit(solution)/shard_map/ppermute | solution.py:24
  19.9 1.7 %copy-start = (s32[16,255]{1,0:T(8,128)S(1)}, s32[16,255]{1,0:T(8,128)}, u32[]{:S(2)}) copy-start(s32[16,255]{1,0:T(8,128)} %param.11) | copy-start | bytes 48964
  19.9 2.0 %copy-start.2 = (bf16[255]{0:T(256)(128)(2,1)S(1)}, bf16[255]{0:T(256)(128)(2,1)}, u32[]{:S(2)}) copy-start(bf16[255]{0:T(256)(128)(2,1)} %param.10) | copy-start | bytes 1534
  23.5 1.5 %copy-start.3 = (f32[32]{0:T(128)S(1)}, f32[32]{0:T(128)}, u32[]{:S(2)}) copy-start(f32[32]{0:T(128)} %param.9) | copy-start | bytes 388

commit v3 on v2

--- a/solution.py
+++ b/solution.py
@@ -52,13 +52,15 @@
     chans = own_ref.shape[2]
     blocks = chans // BLOCK
     width = 2 * BLOCK
+    owns = []
     for block in range(blocks):
         own = own_ref[0, :, block * BLOCK : (block + 1) * BLOCK]
-        own = (own.astype(jnp.float32) * (1.0 / F)).T.astype(jnp.bfloat16)
-        start = (blocks - 1 - block) * BLOCK
-        for lag in range(2 * SMAX + 1):
+        owns.append((own.astype(jnp.float32) * (1.0 / F)).T.astype(jnp.bfloat16))
+    for lag in range(2 * SMAX + 1):
+        for block in range(blocks):
+            start = (blocks - 1 - block) * BLOCK
             partner = ext_ref[time + lag, :, start : start + 3 * BLOCK]
-            products = jnp.dot(own, partner, preferred_element_type=jnp.float32)
+            products = jnp.dot(owns[block], partner, preferred_element_type=jnp.float32)
             skewed = pltpu.roll(products, 0, 1, stride=1, stride_axis=0)
             band_ref[block * BLOCK : (block + 1) * BLOCK, lag * width : (lag + 1) * width] = skewed[
                 :, BLOCK:

time: 67.9 us -> 67.6 us (level)
  no operation moved by 1% of the time
where the time goes in v3:
time: 67.6 us; the launch traced here: 67.3 us
  Pallas kernels  39.7 us (59%)
  starting transfers between devices  10.5 us (16%)
  local copies, waits for them, and re-layouts  9.07 us (13%)
  waiting for transfers between devices  3.31 us (5%)
  other arithmetic  2.78 us (4%)
  matrix products  1.59 us (2%)
    pallas_call x1, Pallas kernels, body(): pl.pallas_call(correlate_kernel, grid=(local_times,), in_specs=[pl.BlockS...  39.7 us
    ppermute x2, starting transfers between devices, extended_2(): after = lax.ppermute(first, axis, down)  7.29 us
    ppermute x2, waiting for transfers between devices, extended_2(): before = lax.ppermute(last, axis, up)  3.3 us
    ppermute x2, starting transfers between devices, extended_2(): before = lax.ppermute(last, axis, up)  3.21 us
    unnamed x32, local copies, waits for them, and re-layouts  2.81 us
    gather x2, local copies, waits for them, and re-layouts, body(): jnp.take(raw_samples, local_index, axis=1).reshape(-1, 2, local_chans)  2.01 us
    dot_general x1, local copies, waits for them, and re-layouts, encode_region(): summed = jnp.dot(spread, patches, preferred_element_type=jnp.float32)  1.57 us
  transfers between devices with their start and end apart: 4, of which 1 were waited for; matrix products, arithmetic and copies ran while one was open for 7% of the time, Pallas kernels for 0%

profile of v3, /device:TPU:26, one launch (start us, length us, event | category | flops | bytes accessed | tf_op | source)
XLA Modules:
  0.0 67.3 jit_solution(16069965280707185704)
XLA Ops:
  0.0 1.0 %copy.25 = bf16[32,768]{0,1:T(8,128)(2,1)S(1)} copy(bf16[32,768]{1,0:T(8,128)(2,1)} %param.6) | data formatting | bytes 98304 | tf_op args[0]
  1.0 0.7 %broadcast_subtract_fusion = s32[768]{0:T(1024)S(1)} fusion(s32[768]{0:T(1024)} %param.7, s32[]{:T(128)S(6)} %mul.21), kind=kLoop, calls=%fused_computation.70 | loop fusion | flops 768 | bytes 6148 | tf_op jit(solution)/shard_map/sub | solution.py:93
  1.7 0.2 reshape.145
  2.1 1.9 %gather_fusion = bf16[768,32]{1,0:T(8,128)(2,1)S(1)} fusion(bf16[32,768]{0,1:T(8,128)(2,1)S(1)} %copy.25, s32[1024]{0:T(1024)S(1)} %pad_clamp_fusion), kind=kCustom, calls=%fused_computation | custom fusion | bytes 101376 | tf_op jit(solution)/shard_map/jit(_take)/gather | solution.py:95
  4.0 0.1 copy.27
  4.1 0.1 copy.23
  4.3 2.7 %collective-permute-start.1 = (bf16[32,2,129]{2,0,1:T(8,128)(2,1)S(1)}, bf16[32,2,129]{2,0,1:T(8,128)(2,1)S(1)}, u32[]{:S(2)}, u32[]{:S(2)}) collective-permute-start(bf16[32,2,129]{2,0,1:T(8,128)(2,1)S(1)} %get-tuple-element.10), channel_id=1, source_target_pairs={{2,0},{4,2},{6,4},{8,6},{10,8},{12,10},{14,12},{16,14},{18,16},{20... | collective-permute-start | bytes 49544 | tf_op jit(solution)/shard_map/ppermute | solution.py:24
  7.1 1.9 %collective-permute-start = (bf16[32,2,129]{2,0,1:T(8,128)(2,1)S(1)}, bf16[32,2,129]{2,0,1:T(8,128)(2,1)S(1)}, u32[]{:S(2)}, u32[]{:S(2)}) collective-permute-start(bf16[32,2,129]{2,0,1:T(8,128)(2,1)S(1)} %get-tuple-element.9), channel_id=1, source_target_pairs={{0,2},{2,4},{4,6},{6,8},{8,10},{10,12},{12,14},{14,16},{16,18},{18... | collective-permute-start | bytes 49544 | tf_op jit(solution)/shard_map/ppermute | solution.py:23
  9.1 0.1 copy.20
  9.3 0.5 fusion.3
  9.9 3.3 %collective-permute-done = bf16[32,2,129]{2,0,1:T(8,128)(2,1)S(1)} collective-permute-done((bf16[32,2,129]{2,0,1:T(8,128)(2,1)S(1)}, bf16[32,2,129]{2,0,1:T(8,128)(2,1)S(1)}, u32[]{:S(2)}, u32[]{:S(2)}) %collective-permute-start) | collective-permute-done | bytes 16544 | tf_op jit(solution)/shard_map/ppermute | solution.py:23
  13.3 1.3 %collective-permute-start.2 = (bf16[20,2,642]{2,0,1:T(8,128)(2,1)S(1)}, bf16[20,2,642]{2,0,1:T(8,128)(2,1)S(1)}, u32[]{:S(2)}, u32[]{:S(2)}) collective-permute-start(bf16[20,2,642]{2,0,1:T(8,128)(2,1)S(1)} %get-tuple-element.7), channel_id=1, source_target_pairs={{0,1},{2,3},{4,5},{6,7},{8,9},{10,11},{12,13},{14,15},{16,17},{18,... | collective-permute-start | bytes 154088 | tf_op jit(solution)/shard_map/ppermute | solution.py:23
  14.6 4.5 %collective-permute-start.3 = (bf16[20,2,642]{2,0,1:T(8,128)(2,1)S(1)}, bf16[20,2,642]{2,0,1:T(8,128)(2,1)S(1)}, u32[]{:S(2)}, u32[]{:S(2)}) collective-permute-start(bf16[20,2,642]{2,0,1:T(8,128)(2,1)S(1)} %get-tuple-element.8), channel_id=1, source_target_pairs={{1,0},{3,2},{5,4},{7,6},{9,8},{11,10},{13,12},{15,14},{17,16},{19,... | collective-permute-start | bytes 154088 | tf_op jit(solution)/shard_map/ppermute | solution.py:24
  19.2 0.7 %copy.22 = bf16[16,32,9,40]{3,2,1,0:T(8,128)(2,1)S(1)} copy(bf16[16,32,9,40]{3,1,2,0:T(8,128)(2,1)S(1)} %fusion.3) | data formatting | bytes 737280 | tf_op jit(solution)/shard_map/convert_element_type | solution.py:84
  19.9 1.6 %dot_general.13 = bf16[16,32,360]{2,1,0:T(8,128)(2,1)S(1)} reshape(bf16[16,32,9,40]{3,2,1,0:T(8,128)(2,1)S(1)} %copy.22) | data formatting | bytes 737280 | tf_op jit(solution)/shard_map/dot_general | solution.py:85
  21.6 0.2 reverse
  21.8 0.1 copy.33
  22.0 0.1 reverse.1
  22.3 1.2 %fusion.weight_ref = bf16[4352,16]{1,0:T(8,128)(2,1)S(1)} fusion(s32[4352]{0:T(1024)S(1)} %eq.46, s32[256,16]{1,0:T(8,128)S(1)} %pad.13.clone, bf16[4352]{0:T(1024)(128)(2,1)S(1)} %broadcast_in_dim.56), kind=kLoop, calls=%fused_computation.2 | loop fusion | flops 139264 | bytes 181760 | tf_op jit(solution)/shard_map/jit(_where)/select_n | solution.py:34
  23.5 0.1 maximum_maximum_fusion
  23.7 0.1 fusion.17
  24.0 0.1 fusion.14
  24.1 0.1 fusion.13
  24.2 0.1 fusion.12
  24.9 0.1 fusion.11
  25.0 0.5 fusion.5
  25.5 0.5 fusion.4
  26.1 0.3 maximum_select_fusion
  26.4 0.2 slice.138.own_ref
  26.6 0.1 pad.12.raw_ref
  26.7 39.7 %shard_map.64 = f32[16,16,384]{2,1,0:T(8,128)S(1)} custom-call(bf16[16,32,384]{2,1,0:T(8,128)(2,1)S(1)} %slice.138.own_ref, bf16[32,32,640]{2,1,0:T(8,128)(2,1)S(1)} %pad.12.raw_ref, bf16[4352,16]{1,0:T(8,128)(2,1)S(1)} %fusion.weight_ref), custom_call_target="tpu_custom_call" | custom-call | tf_op jit(solution)/shard_map/pallas_call | solution.py:117
  66.4 0.9 %copy.29 = f32[16,16,384]{2,1,0:T(8,128)} copy(f32[16,16,384]{2,0,1:T(8,128)S(1)} %bitcast.109) | data formatting | bytes 786432 | tf_op jit(solution)/shard_map/transpose | solution.py:133
  (47 shorter events, 1.8 us)
Async XLA Ops:
  0.0 9.1 %copy-start.1 = (bf16[32,81]{1,0:T(8,128)(2,1)S(1)}, bf16[32,81]{1,0:T(8,128)(2,1)}, u32[]{:S(2)}) copy-start(bf16[32,81]{1,0:T(8,128)(2,1)} %param.8) | copy-start | bytes 15556
  4.3 5.6 %collective-permute-start.1 = (bf16[32,2,129]{2,0,1:T(8,128)(2,1)S(1)}, bf16[32,2,129]{2,0,1:T(8,128)(2,1)S(1)}, u32[]{:S(2)}, u32[]{:S(2)}) collective-permute-start(bf16[32,2,129]{2,0,1:T(8,128)(2,1)S(1)} %get-tuple-element.10), channel_id=1, source_target_pairs={{2,0},{4,2},{6,4},{8,6},{10,8},{12,10},{14,12},{16,14},{18,16},{20... | collective-permute-start | bytes 49544 | tf_op jit(solution)/shard_map/ppermute | solution.py:24
  7.1 6.1 %collective-permute-start = (bf16[32,2,129]{2,0,1:T(8,128)(2,1)S(1)}, bf16[32,2,129]{2,0,1:T(8,128)(2,1)S(1)}, u32[]{:S(2)}, u32[]{:S(2)}) collective-permute-start(bf16[32,2,129]{2,0,1:T(8,128)(2,1)S(1)} %get-tuple-element.9), channel_id=1, source_target_pairs={{0,2},{2,4},{4,6},{6,8},{8,10},{10,12},{12,14},{14,16},{16,18},{18... | collective-permute-start | bytes 49544 | tf_op jit(solution)/shard_map/ppermute | solution.py:23
  13.3 10.1 %collective-permute-start.2 = (bf16[20,2,642]{2,0,1:T(8,128)(2,1)S(1)}, bf16[20,2,642]{2,0,1:T(8,128)(2,1)S(1)}, u32[]{:S(2)}, u32[]{:S(2)}) collective-permute-start(bf16[20,2,642]{2,0,1:T(8,128)(2,1)S(1)} %get-tuple-element.7), channel_id=1, source_target_pairs={{0,1},{2,3},{4,5},{6,7},{8,9},{10,11},{12,13},{14,15},{16,17},{18,... | collective-permute-start | bytes 154088 | tf_op jit(solution)/shard_map/ppermute | solution.py:23
  14.6 8.8 %collective-permute-start.3 = (bf16[20,2,642]{2,0,1:T(8,128)(2,1)S(1)}, bf16[20,2,642]{2,0,1:T(8,128)(2,1)S(1)}, u32[]{:S(2)}, u32[]{:S(2)}) collective-permute-start(bf16[20,2,642]{2,0,1:T(8,128)(2,1)S(1)} %get-tuple-element.8), channel_id=1, source_target_pairs={{1,0},{3,2},{5,4},{7,6},{9,8},{11,10},{13,12},{15,14},{17,16},{19,... | collective-permute-start | bytes 154088 | tf_op jit(solution)/shard_map/ppermute | solution.py:24
  19.9 1.7 %copy-start = (s32[16,255]{1,0:T(8,128)S(1)}, s32[16,255]{1,0:T(8,128)}, u32[]{:S(2)}) copy-start(s32[16,255]{1,0:T(8,128)} %param.11) | copy-start | bytes 48964
  19.9 2.0 %copy-start.2 = (bf16[255]{0:T(256)(128)(2,1)S(1)}, bf16[255]{0:T(256)(128)(2,1)}, u32[]{:S(2)}) copy-start(bf16[255]{0:T(256)(128)(2,1)} %param.10) | copy-start | bytes 1534
  23.5 1.5 %copy-start.3 = (f32[32]{0:T(128)S(1)}, f32[32]{0:T(128)}, u32[]{:S(2)}) copy-start(f32[32]{0:T(128)} %param.9) | copy-start | bytes 388
